TPU v7x, 128 devices: a whole 4x4x4 slice. The times are simulated.
128 devices in a mesh: dp: 128 (over z, y, x, core).
Axes of the slice: x: 4, y: 4, z: 4, core: 2. Of those that a mesh axis runs over, the one named last changes fastest.
Arguments:
- tokens: bfloat16 [2, 16384, 960], P(None, 'dp'), may hold values from -6 to 6
- segment_ids: int32 [2, 16384], P(None, 'dp'), may hold values from 0 to 128, as said below
- attn_weight: bfloat16 [2560, 960], P('dp'), may hold values from -0.25 to 0.25
- gate_up: bfloat16 [2, 2560, 960], P(None, 'dp'), may hold values from -0.1875 to 0.1875
- down_weight: bfloat16 [2560, 960], P('dp'), may hold values from -0.125 to 0.125
- norm_gains: bfloat16 [1920], P('dp'), may hold values from 0.5 to 1.5
- cotangent: bfloat16 [2, 16384, 960], P(None, 'dp'), may hold values from -6 to 6
Outputs:
- layer_output: bfloat16 [2, 16384, 960], P(None, 'dp')
- input_grad: bfloat16 [2, 16384, 960], P(None, 'dp')
- attn_grad: float32 [2560, 960], P('dp')
- gate_up_grad: float32 [2, 2560, 960], P(None, 'dp')
- down_grad: float32 [2560, 960], P('dp')
- gains_grad: float32 [1920], P('dp')
Inputs may be any that keep to these rules, and one draw needn't show every extreme that they name: `segment_ids`: within each micro-batch every aligned block of 128 slots (one device's slots) holds whole sequences numbered 0, 1, 2, ... in order, never falling; slots numbered 128 are padding at the block's end; every block is at least half full, and in every draw some block is one sequence of 128 tokens.
All inputs are finite; a program needn't handle non-finite values.
Results may differ from a plain program's by a relative error of at most 0.015.
Values may be sent and summed in bfloat16 or wider, within the bound.
No kernel may reach another device: no remote copies, remote signals or barrier semaphores. Data moves between devices by JAX's collectives and lax.ppermute only.
A program may use at most 192 MiB of HBM per device.

v0:
```python
import jax
import jax.numpy as jnp
from jax import lax
from jax.sharding import PartitionSpec as P

HEADS = 15
KV_HEADS = 5
HEAD_DIM = 64
MICRO = 2


EPS = 1e-05
THETA = 100000.0
NEG_FILL = -1e30


def rope_tables(seg_row):
    count = seg_row.shape[0]
    places = jnp.arange(count)
    allowed = (seg_row[:, None] == seg_row[None, :]) & (places[None, :] <= places[:, None])
    position = jnp.sum(allowed.astype(jnp.float32), axis=-1) - 1.0
    freqs = THETA ** (-2.0 * jnp.arange(HEAD_DIM // 2).astype(jnp.float32) / HEAD_DIM)
    angles = position[:, None] * freqs[None, :]
    return (jnp.cos(angles), jnp.sin(angles), allowed)


def rotate(values, cosine_table, sine_table):
    half_dim = values.shape[-1] // 2
    former = values[..., :half_dim]
    latter = values[..., half_dim:]
    cosine = cosine_table[:, None, :]
    sine = sine_table[:, None, :]
    return jnp.concatenate(
        [former * cosine - latter * sine, latter * cosine + former * sine], axis=-1
    )


def unrotate(values, cosine_table, sine_table):
    half_dim = values.shape[-1] // 2
    former = values[..., :half_dim]
    latter = values[..., half_dim:]
    cosine = cosine_table[:, None, :]
    sine = sine_table[:, None, :]
    return jnp.concatenate(
        [former * cosine + latter * sine, latter * cosine - former * sine], axis=-1
    )


def inv_rms(values):
    return lax.rsqrt(jnp.mean(values * values, axis=-1, keepdims=True) + EPS)


def norm_back(grad_normed, source, inverse, gain_vec):
    scaled = source * inverse
    grad_scaled = grad_normed * gain_vec
    grad_gain = jnp.sum(grad_normed * scaled, axis=0)
    grad_source = inverse * (
        grad_scaled - scaled * jnp.mean(grad_scaled * scaled, axis=-1, keepdims=True)
    )
    return (grad_source, grad_gain)


def contract_rows(left, right):
    return lax.dot_general(
        left, right, (((0,), (0,)), ((), ())), preferred_element_type=jnp.float32
    )


def contract_cols(left, right):
    return lax.dot_general(
        left, right, (((1,), (1,)), ((), ())), preferred_element_type=jnp.float32
    )


def forward_pass(weights, token_block, seg_row):
    attn_full, gate_full, down_full, gain_full = weights
    count, width = token_block.shape
    kv_width = KV_HEADS * HEAD_DIM
    qkv_rows = width + 2 * kv_width
    group = HEADS // KV_HEADS
    inputs = token_block.astype(jnp.float32)
    live_rows = (seg_row < count).astype(jnp.float32)[:, None]
    gain_attn = gain_full[:width].astype(jnp.float32)
    gain_mlp = gain_full[width:].astype(jnp.float32)
    scale_one = inv_rms(inputs)
    normed_one = (inputs * scale_one * gain_attn).astype(jnp.bfloat16)
    projected = contract_cols(normed_one, attn_full[:qkv_rows])
    cosine_table, sine_table, allowed = rope_tables(seg_row)
    queries = rotate(projected[:, :width].reshape(count, HEADS, HEAD_DIM), cosine_table, sine_table)
    queries = queries.astype(jnp.bfloat16).reshape(count, KV_HEADS, group, HEAD_DIM)
    keys_rot = rotate(
        projected[:, width : width + kv_width].reshape(count, KV_HEADS, HEAD_DIM),
        cosine_table,
        sine_table,
    )
    keys_rot = keys_rot.astype(jnp.bfloat16)
    values = (
        projected[:, width + kv_width :].reshape(count, KV_HEADS, HEAD_DIM).astype(jnp.bfloat16)
    )
    scores = jnp.einsum("qkgd,tkd->kgqt", queries, keys_rot, preferred_element_type=jnp.float32)
    scores = jnp.where(allowed, scores * HEAD_DIM ** (-0.5), NEG_FILL)
    row_max = jnp.max(scores, axis=-1, keepdims=True)
    expd = jnp.exp(scores - row_max)
    total = jnp.sum(expd, axis=-1, keepdims=True)
    probs = (expd / total).astype(jnp.bfloat16)
    log_total = row_max + jnp.log(total)
    attended = jnp.einsum("kgqt,tkd->qkgd", probs, values, preferred_element_type=jnp.float32)
    attended = attended.reshape(count, width).astype(jnp.bfloat16)
    branch_attn = jnp.dot(attended, attn_full[qkv_rows:], preferred_element_type=jnp.float32)
    hidden_res = inputs + live_rows * branch_attn
    scale_two = inv_rms(hidden_res)
    normed_two = (hidden_res * scale_two * gain_mlp).astype(jnp.bfloat16)
    gate_and_up = jnp.einsum(
        "rd,cfd->crf", normed_two, gate_full, preferred_element_type=jnp.float32
    )
    gate_vals = gate_and_up[0]
    up_vals = gate_and_up[1]
    product = (gate_vals * jax.nn.sigmoid(gate_vals) * up_vals).astype(jnp.bfloat16)
    branch_mlp = jnp.dot(product, down_full, preferred_element_type=jnp.float32)
    result = (hidden_res + live_rows * branch_mlp).astype(jnp.bfloat16)
    kept = (
        inputs,
        live_rows,
        scale_one,
        normed_one,
        queries,
        keys_rot,
        values,
        allowed,
        log_total,
        attended,
        hidden_res,
        scale_two,
        normed_two,
        gate_vals,
        up_vals,
        product,
        cosine_table,
        sine_table,
    )
    return (result, kept)


def backward_pass(weights, kept, cot_block):
    attn_full, gate_full, down_full, gain_full = weights
    (
        inputs,
        live_rows,
        scale_one,
        normed_one,
        queries,
        keys_rot,
        values,
        allowed,
        log_total,
        attended,
        hidden_res,
        scale_two,
        normed_two,
        gate_vals,
        up_vals,
        product,
        cosine_table,
        sine_table,
    ) = kept
    count, width = inputs.shape
    kv_width = KV_HEADS * HEAD_DIM
    qkv_rows = width + 2 * kv_width
    group = HEADS // KV_HEADS
    gain_attn = gain_full[:width].astype(jnp.float32)
    gain_mlp = gain_full[width:].astype(jnp.float32)
    grad_out = cot_block.astype(jnp.float32)
    grad_mlp = (live_rows * grad_out).astype(jnp.bfloat16)
    grad_down = contract_rows(product, grad_mlp)
    grad_prod = contract_cols(grad_mlp, down_full)
    sigma = jax.nn.sigmoid(gate_vals)
    grad_gate = grad_prod * up_vals * sigma * (1.0 + gate_vals * (1.0 - sigma))
    grad_up = grad_prod * gate_vals * sigma
    grad_pair = jnp.stack([grad_gate, grad_up]).astype(jnp.bfloat16)
    grad_gate_up = jnp.einsum(
        "crf,rd->cfd", grad_pair, normed_two, preferred_element_type=jnp.float32
    )
    grad_normed_two = jnp.einsum(
        "crf,cfd->rd", grad_pair, gate_full, preferred_element_type=jnp.float32
    )
    grad_hidden, grad_gain_mlp = norm_back(grad_normed_two, hidden_res, scale_two, gain_mlp)
    grad_hidden = grad_out + grad_hidden
    grad_branch = (live_rows * grad_hidden).astype(jnp.bfloat16)
    grad_outproj = contract_rows(attended, grad_branch)
    grad_att = contract_cols(grad_branch, attn_full[qkv_rows:]).astype(jnp.bfloat16)
    grad_att = grad_att.reshape(count, KV_HEADS, group, HEAD_DIM)
    scores = jnp.einsum("qkgd,tkd->kgqt", queries, keys_rot, preferred_element_type=jnp.float32)
    scores = jnp.where(allowed, scores * HEAD_DIM ** (-0.5), NEG_FILL)
    probs = jnp.exp(scores - log_total)
    grad_probs = jnp.einsum("qkgd,tkd->kgqt", grad_att, values, preferred_element_type=jnp.float32)
    delta = jnp.sum(probs * grad_probs, axis=-1, keepdims=True)
    grad_scores = (HEAD_DIM ** (-0.5) * probs * (grad_probs - delta)).astype(jnp.bfloat16)
    grad_queries = jnp.einsum(
        "kgqt,tkd->qkgd", grad_scores, keys_rot, preferred_element_type=jnp.float32
    )
    grad_keys = jnp.einsum(
        "kgqt,qkgd->tkd", grad_scores, queries, preferred_element_type=jnp.float32
    )
    grad_values = jnp.einsum(
        "kgqt,qkgd->tkd", probs.astype(jnp.bfloat16), grad_att, preferred_element_type=jnp.float32
    )
    grad_queries = unrotate(grad_queries.reshape(count, HEADS, HEAD_DIM), cosine_table, sine_table)
    grad_keys = unrotate(grad_keys, cosine_table, sine_table)
    grad_proj = jnp.concatenate(
        [
            grad_queries.reshape(count, width),
            grad_keys.reshape(count, kv_width),
            grad_values.reshape(count, kv_width),
        ],
        axis=1,
    ).astype(jnp.bfloat16)
    grad_qkv = contract_rows(grad_proj, normed_one)
    grad_normed_one = jnp.dot(grad_proj, attn_full[:qkv_rows], preferred_element_type=jnp.float32)
    grad_inputs, grad_gain_attn = norm_back(grad_normed_one, inputs, scale_one, gain_attn)
    grad_inputs = grad_hidden + grad_inputs
    grads = (
        jnp.concatenate([grad_qkv, grad_outproj], axis=0),
        grad_gate_up,
        grad_down,
        jnp.concatenate([grad_gain_attn, grad_gain_mlp], axis=0),
    )
    return (grads, grad_inputs.astype(jnp.bfloat16))


def body(tokens, segment_ids, attn_weight, gate_up, down_weight, norm_gains, cotangent):
    outputs = []
    input_grads = []
    grad_total = None
    for micro_index in range(MICRO):
        gathered = (
            lax.all_gather(attn_weight, "dp", axis=0, tiled=True),
            lax.all_gather(gate_up, "dp", axis=1, tiled=True),
            lax.all_gather(down_weight, "dp", axis=0, tiled=True),
            lax.all_gather(norm_gains, "dp", axis=0, tiled=True),
        )
        result, kept = forward_pass(gathered, tokens[micro_index], segment_ids[micro_index])
        gathered = (
            lax.all_gather(attn_weight, "dp", axis=0, tiled=True),
            lax.all_gather(gate_up, "dp", axis=1, tiled=True),
            lax.all_gather(down_weight, "dp", axis=0, tiled=True),
            lax.all_gather(norm_gains, "dp", axis=0, tiled=True),
        )
        grads, grad_inputs = backward_pass(gathered, kept, cotangent[micro_index])
        grad_total = grads if micro_index == 0 else jax.tree.map(jnp.add, grad_total, grads)
        outputs.append(result)
        input_grads.append(grad_inputs)
    grad_attn, grad_gate, grad_down, grad_gain = (
        lax.psum_scatter(grad_total[0], "dp", scatter_dimension=0, tiled=True),
        lax.psum_scatter(grad_total[1], "dp", scatter_dimension=1, tiled=True),
        lax.psum_scatter(grad_total[2], "dp", scatter_dimension=0, tiled=True),
        lax.psum_scatter(grad_total[3], "dp", scatter_dimension=0, tiled=True),
    )
    return (jnp.stack(outputs), jnp.stack(input_grads), grad_attn, grad_gate, grad_down, grad_gain)


def solution(mesh):
    return jax.shard_map(
        body,
        mesh=mesh,
        in_specs=(
            P(None, "dp", None),
            P(None, "dp"),
            P("dp", None),
            P(None, "dp", None),
            P("dp", None),
            P("dp"),
            P(None, "dp", None),
        ),
        out_specs=(
            P(None, "dp", None),
            P(None, "dp", None),
            P("dp", None),
            P(None, "dp", None),
            P("dp", None),
            P("dp"),
        ),
        check_vma=False,
    )
```

profile of v0, /device:TPU:0, one launch (start us, length us, event | category | flops | bytes accessed | tf_op | source)
XLA Modules:
  0.0 917.5 jit_solution(17436766049935484618)
XLA Ops:
  10.3 69.2 %all-reduce = bf16[1920]{0:T(1024)(128)(2,1)S(1)} all-reduce(bf16[1920]{0:T(1024)(128)(2,1)S(1)} %dynamic-update-slice), channel_id=1, replica_groups=mesh['dp'=128] {'dp'}, use_global_device_ids=true, to_apply=%add | all-reduce | flops 1920 | bytes 7680
  84.6 4.5 slice.160
  89.1 5.2 reshape.320
  99.8 3.4 slice.169
  103.2 4.1 reshape.321
  107.3 44.0 %all-gather.10.cloned.1.call-done = bf16[128,20,960]{2,1,0:T(8,128)(2,1)} async-done(((bf16[1,20,960]{2,1,0:T(8,128)(2,1)}), bf16[128,20,960]{2,1,0:T(8,128)(2,1)}) %all-gather.10.cloned.1.call-update) | async-done | bytes 4915216 | tf_op jit(solution)/shard_map/all_gather | solution.py:238
  151.3 9.8 %reshape.319 = bf16[2560,960]{1,0:T(8,128)(2,1)} reshape(bf16[128,20,960]{2,1,0:T(8,128)(2,1)} %all-gather.10.cloned.1.call-done) | data formatting | bytes 9830400
  172.9 50.8 %all-gather.6.cloned.1.call-done = bf16[2,2560,960]{2,0,1:T(2,128)(2,1)} async-done(((bf16[2,20,960]{2,0,1:T(2,128)(2,1)}), bf16[2,2560,960]{2,0,1:T(2,128)(2,1)}) %all-gather.6.cloned.1.call-update) | async-done | bytes 9830416 | tf_op jit(solution)/shard_map/all_gather | solution.py:237
  223.7 10.3 %fusion.9 = f32[2,128,2560]{2,1,0:T(8,128)S(1)} fusion(bf16[2,2560,960]{2,0,1:T(2,128)(2,1)} %all-gather.6.cloned.1.call-done, f32[128,960]{0,1:T(8,128)} %get-tuple-element.83, f32[960]{0:T(1024)} %get-tuple-element.64, f32[128]{0:T(128)} %add_rsqrt_fusion.2), kind=kOutput, calls=%fused_computation.11 | convolution fusion | flops 1258659840 | bytes 12947712 | tf_op jit(solution)/shard_map/rd,cfd->crf/dot_general | solution.py:113
  234.1 5.6 fusion.77
  239.8 10.5 %fusion.12 = f32[2,128,2560]{2,1,0:T(8,128)S(1)} fusion(bf16[2,2560,960]{2,0,1:T(2,128)(2,1)} %all-gather.6.cloned.1.call-done, f32[128,960]{0,1:T(8,128)S(1)} %copy-done.18, f32[128]{0:T(128)S(1)} %copy-done.93, f32[960]{0:T(1024)S(1)} %copy-done.76), kind=kOutput, calls=%fused_computation.12 | convolution fusion | flops 1258659840 | bytes 12947712 | tf_op jit(solution)/shard_map/rd,cfd->crf/dot_general | solution.py:113
  252.6 9.0 fusion.46
  261.6 10.3 %multiply_reduce_fusion.3 = (f32[960]{0:T(1024)}, f32[128]{0:T(128)S(1)}, f32[128]{0:T(128)S(1)}, f32[960]{0:T(1024)}, f32[128,960]{0,1:T(8,128)S(1)}) fusion(f32[128,960]{0,1:T(8,128)S(1)} %copy-done.16, f32[128]{0:T(128)S(1)} %copy-done.92, f32[960]{0:T(1024)S(1)} %copy-done.76, f32[128,960]{0,1:T(8,128)S(1)} %fusion.46, f32[128,960]{0,1:T(8,128)S(1)} %copy-done.18, ...), kind=kOutput, calls=%fused_computation.148 | convolution fusion | flops 1260418816 | bytes 13120768 | tf_op jit(solution)/shard_map/crf,cfd->rd/dot_general | solution.py:183
  283.2 8.7 fusion.57
  292.1 13.5 %convolution_add_fusion = f32[2,2560,960]{2,1,0:T(8,128)} fusion(f32[2,2560,960]{2,1,0:T(8,128)} %fusion.57, bf16[1,128,2560]{2,1,0:T(8,128)(2,1)} %copy-done.34, bf16[1,128,2560]{2,1,0:T(8,128)(2,1)} %copy-done.33, f32[128,960]{0,1:T(8,128)S(1)} %copy-done.18, f32[128]{0:T(128)S(1)} %copy-done.94, f32[960]{0:T(1024)S(1)} %copy-done.77), kind=kOutput, calls=%fused_computation | convolution fusion | flops 1264230400 | bytes 41128192 | tf_op jit(solution)/shard_map/crf,rd->cfd/dot_general | solution.py:180
  305.7 35.5 %copy.53 = f32[2,2560,960]{2,0,1:T(2,128)} copy(f32[2,2560,960]{2,1,0:T(8,128)} %convolution_add_fusion) | data formatting | bytes 39321600 | tf_op jit(solution)/shard_map/add | solution.py:249
  344.6 6.0 maximum_add_fusion
  351.3 3.5 fusion.71
  354.8 6.4 convolution_add_fusion.1
  361.1 383.0 %fusion = f32[24,960]{1,0:T(8,128)} fusion(f32[2560,960]{1,0:T(8,128)} %convolution_add_fusion.1), kind=kCustom, calls=%all-reduce-scatter | all-reduce-scatter fusion | flops 2949121 | bytes 9922560
  755.9 4.8 fusion.51
  766.1 17.4 %collective-permute-start.14 = (f32[24,960]{1,0:T(8,128)S(1)}, f32[24,960]{1,0:T(8,128)S(1)}, u32[]{:S(2)}, u32[]{:S(2)}) collective-permute-start(f32[24,960]{1,0:T(8,128)S(1)} %copy-done.43), channel_id=1, source_target_pairs={{0,15},{1,16},{2,17},{3,18},{4,19},{5,20},{6,21},{7,22},{8,23},{9,... | collective-permute-start | bytes 276488
  783.5 2.8 collective-permute-start.13
  787.8 4.6 collective-permute-start.11
  793.8 66.3 %all-reduce.4 = f32[1920]{0:T(1024)S(1)} all-reduce(f32[1920]{0:T(1024)S(1)} %maximum_add_fusion.1), channel_id=5, replica_groups=mesh['dp'=128] {'dp'}, use_global_device_ids=true, to_apply=%region_23.24.clone | all-reduce | flops 1920 | bytes 15360
  864.2 3.9 collective-permute-start.7
  868.1 5.8 collective-permute-start.6
  873.9 3.3 collective-permute-start.5
  880.2 4.3 collective-permute-start.3
  885.8 4.0 collective-permute-start.1
  889.9 3.3 collective-permute-start
  895.3 10.7 %concatenate.80 = f32[532,960]{1,0:T(8,128)S(1)} concatenate(f32[4,960]{1,0:T(4,128)S(1)} %collective-permute-done.21, f32[24,960]{1,0:T(8,128)} %copy-done.68, f32[24,960]{1,0:T(8,128)} %copy-done.69, f32[24,960]{1,0:T(8,128)} %copy-done.70, f32[24,960]{1,0:T(8,128)} %copy-done.71, f32[24,960]{1,0:T(8,128)S(1)} %collective-permute-done.16, ...), dimensions={0} | concatenate | bytes 4085760
  (327 shorter events, 76.9 us)
Async XLA Ops:
  7.2 77.5 %all-gather.8.cloned.1.call-start = ((), (), s32[]{:S(2)}) async-start(), calls=%async_computation.1 | async-start | bytes 6340608 | tf_op jit(solution)/shard_map/all_gather | solution.py:236
  7.9 143.4 %all-gather.10.cloned.1.call-start = ((), (), s32[]{:S(2)}) async-start(), calls=%async_computation.2 | async-start | bytes 6340608 | tf_op jit(solution)/shard_map/all_gather | solution.py:238
  8.6 215.1 %all-gather.6.cloned.1.call-start = ((), (), s32[]{:S(2)}) async-start(), calls=%async_computation | async-start | bytes 10567680 | tf_op jit(solution)/shard_map/all_gather | solution.py:237
  9.4 897.3 %all-reduce.9.cloned.1.call-start = ((), (), s32[]{:S(2)}) async-start(), calls=%async_computation.3 | async-start | bytes 61603840
  84.6 76.5 %copy-start.44 = (f32[128,32]{0,1:T(8,128)}, f32[128,32]{0,1:T(8,128)S(1)}, u32[]{:S(2)}) copy-start(f32[128,32]{0,1:T(8,128)S(1)} %get-tuple-element.74) | copy-start | bytes 49156
  84.6 76.5 %copy-start.46 = (f32[128,32]{0,1:T(8,128)}, f32[128,32]{0,1:T(8,128)S(1)}, u32[]{:S(2)}) copy-start(f32[128,32]{0,1:T(8,128)S(1)} %get-tuple-element.75) | copy-start | bytes 49156
  274.9 67.6 %copy-start.28 = (bf16[5,64,128]{2,1,0:T(8,128)(2,1)}, bf16[5,64,128]{2,1,0:T(8,128)(2,1)S(1)}, u32[]{:S(2)}) copy-start(bf16[5,64,128]{2,1,0:T(8,128)(2,1)S(1)} %fusion.54) | copy-start | bytes 245764
  305.7 35.7 %copy-start.48 = (bf16[5,64,128]{2,1,0:T(8,128)(2,1)S(1)}, bf16[5,64,128]{2,1,0:T(8,128)(2,1)}, u32[]{:S(2)}) copy-start(bf16[5,64,128]{2,1,0:T(8,128)(2,1)} %fusion.53) | copy-start | bytes 245764
  305.7 35.7 %copy-start.67 = (f32[960]{0:T(1024)S(1)}, f32[960]{0:T(1024)}, u32[]{:S(2)}) copy-start(f32[960]{0:T(1024)} %copy-done.66) | copy-start | bytes 11524
  305.7 35.7 %copy-start.88 = (f32[128]{0:T(128)S(1)}, f32[128]{0:T(128)}, u32[]{:S(2)}) copy-start(f32[128]{0:T(128)} %copy-done.87) | copy-start | bytes 1540
  744.9 19.5 %collective-permute-start.20 = (f32[24,960]{1,0:T(8,128)}, f32[24,960]{1,0:T(8,128)S(1)}, u32[]{:S(2)}, u32[]{:S(2)}) collective-permute-start(f32[24,960]{1,0:T(8,128)} %fusion), channel_id=1, source_target_pairs={{0,21},{1,22},{2,23},{3,24},{4,25},{5,26},{6,27},{7,28},{8,29},{9,... | collective-permute-start | bytes 276488
  746.2 19.9 %collective-permute-start.19 = (f32[24,960]{1,0:T(8,128)}, f32[24,960]{1,0:T(8,128)S(1)}, u32[]{:S(2)}, u32[]{:S(2)}) collective-permute-start(f32[24,960]{1,0:T(8,128)} %fusion), channel_id=1, source_target_pairs={{0,20},{1,21},{2,22},{3,23},{4,24},{5,25},{6,26},{7,27},{8,28},{9,... | collective-permute-start | bytes 276488
  747.5 36.0 %collective-permute-start.18 = (f32[24,960]{1,0:T(8,128)}, f32[24,960]{1,0:T(8,128)S(1)}, u32[]{:S(2)}, u32[]{:S(2)}) collective-permute-start(f32[24,960]{1,0:T(8,128)} %fusion), channel_id=1, source_target_pairs={{0,19},{1,20},{2,21},{3,22},{4,23},{5,24},{6,25},{7,26},{8,27},{9,... | collective-permute-start | bytes 276488
  748.8 37.5 %collective-permute-start.17 = (f32[24,960]{1,0:T(8,128)}, f32[24,960]{1,0:T(8,128)S(1)}, u32[]{:S(2)}, u32[]{:S(2)}) collective-permute-start(f32[24,960]{1,0:T(8,128)} %fusion), channel_id=1, source_target_pairs={{0,18},{1,19},{2,20},{3,21},{4,22},{5,23},{6,24},{7,25},{8,26},{9,... | collective-permute-start | bytes 276488
  750.1 13.0 %collective-permute-start.21 = (f32[4,960]{1,0:T(4,128)S(1)}, f32[4,960]{1,0:T(4,128)S(1)}, u32[]{:S(2)}, u32[]{:S(2)}) collective-permute-start(f32[4,960]{1,0:T(4,128)S(1)} %slice.190), channel_id=1, source_target_pairs={{0,22},{1,23},{2,24},{3,25},{4,26},{5,27},{6,28},{7,29},{8,30},{9,... | collective-permute-start | bytes 46088
  763.1 24.6 %collective-permute-start.16 = (f32[24,960]{1,0:T(8,128)S(1)}, f32[24,960]{1,0:T(8,128)S(1)}, u32[]{:S(2)}, u32[]{:S(2)}) collective-permute-start(f32[24,960]{1,0:T(8,128)S(1)} %copy-done.43), channel_id=1, source_target_pairs={{0,17},{1,18},{2,19},{3,20},{4,21},{5,22},{6,23},{7,24},{8,25},{9,... | collective-permute-start | bytes 276488
  764.5 27.9 %collective-permute-start.15 = (f32[24,960]{1,0:T(8,128)S(1)}, f32[24,960]{1,0:T(8,128)S(1)}, u32[]{:S(2)}, u32[]{:S(2)}) collective-permute-start(f32[24,960]{1,0:T(8,128)S(1)} %copy-done.43), channel_id=1, source_target_pairs={{0,16},{1,17},{2,18},{3,19},{4,20},{5,21},{6,22},{7,23},{8,24},{9,... | collective-permute-start | bytes 276488
  766.1 94.6 %collective-permute-start.14 = (f32[24,960]{1,0:T(8,128)S(1)}, f32[24,960]{1,0:T(8,128)S(1)}, u32[]{:S(2)}, u32[]{:S(2)}) collective-permute-start(f32[24,960]{1,0:T(8,128)S(1)} %copy-done.43), channel_id=1, source_target_pairs={{0,15},{1,16},{2,17},{3,18},{4,19},{5,20},{6,21},{7,22},{8,23},{9,... | collective-permute-start | bytes 276488
  783.5 78.9 %collective-permute-start.13 = (f32[24,960]{1,0:T(8,128)S(1)}, f32[24,960]{1,0:T(8,128)S(1)}, u32[]{:S(2)}, u32[]{:S(2)}) collective-permute-start(f32[24,960]{1,0:T(8,128)S(1)} %copy-done.43), channel_id=1, source_target_pairs={{0,14},{1,15},{2,16},{3,17},{4,18},{5,19},{6,20},{7,21},{8,22},{9,... | collective-permute-start | bytes 276488
  786.4 77.8 %collective-permute-start.12 = (f32[24,960]{1,0:T(8,128)S(1)}, f32[24,960]{1,0:T(8,128)S(1)}, u32[]{:S(2)}, u32[]{:S(2)}) collective-permute-start(f32[24,960]{1,0:T(8,128)S(1)} %copy-done.43), channel_id=1, source_target_pairs={{0,13},{1,14},{2,15},{3,16},{4,17},{5,18},{6,19},{7,20},{8,21},{9,... | collective-permute-start | bytes 276488
  787.8 80.3 %collective-permute-start.11 = (f32[24,960]{1,0:T(8,128)S(1)}, f32[24,960]{1,0:T(8,128)S(1)}, u32[]{:S(2)}, u32[]{:S(2)}) collective-permute-start(f32[24,960]{1,0:T(8,128)S(1)} %copy-done.43), channel_id=1, source_target_pairs={{0,12},{1,13},{2,14},{3,15},{4,16},{5,17},{6,18},{7,19},{8,20},{9,... | collective-permute-start | bytes 276488
  792.4 81.5 %collective-permute-start.10 = (f32[24,960]{1,0:T(8,128)S(1)}, f32[24,960]{1,0:T(8,128)S(1)}, u32[]{:S(2)}, u32[]{:S(2)}) collective-permute-start(f32[24,960]{1,0:T(8,128)S(1)} %copy-done.43), channel_id=1, source_target_pairs={{0,11},{1,12},{2,13},{3,14},{4,15},{5,16},{6,17},{7,18},{8,19},{9,... | collective-permute-start | bytes 276488
  860.7 17.3 %collective-permute-start.9 = (f32[24,960]{1,0:T(8,128)S(1)}, f32[24,960]{1,0:T(8,128)S(1)}, u32[]{:S(2)}, u32[]{:S(2)}) collective-permute-start(f32[24,960]{1,0:T(8,128)S(1)} %copy-done.43), channel_id=1, source_target_pairs={{0,10},{1,11},{2,12},{3,13},{4,14},{5,15},{6,16},{7,17},{8,18},{9,... | collective-permute-start | bytes 276488
  862.4 17.7 %collective-permute-start.8 = (f32[24,960]{1,0:T(8,128)S(1)}, f32[24,960]{1,0:T(8,128)S(1)}, u32[]{:S(2)}, u32[]{:S(2)}) collective-permute-start(f32[24,960]{1,0:T(8,128)S(1)} %copy-done.43), channel_id=1, source_target_pairs={{0,9},{1,10},{2,11},{3,12},{4,13},{5,14},{6,15},{7,16},{8,17},{9,1... | collective-permute-start | bytes 276488
  864.2 20.3 %collective-permute-start.7 = (f32[24,960]{1,0:T(8,128)S(1)}, f32[24,960]{1,0:T(8,128)S(1)}, u32[]{:S(2)}, u32[]{:S(2)}) collective-permute-start(f32[24,960]{1,0:T(8,128)S(1)} %copy-done.43), channel_id=1, source_target_pairs={{0,8},{1,9},{2,10},{3,11},{4,12},{5,13},{6,14},{7,15},{8,16},{9,17... | collective-permute-start | bytes 276488
  868.1 17.7 %collective-permute-start.6 = (f32[24,960]{1,0:T(8,128)S(1)}, f32[24,960]{1,0:T(8,128)S(1)}, u32[]{:S(2)}, u32[]{:S(2)}) collective-permute-start(f32[24,960]{1,0:T(8,128)S(1)} %copy-done.43), channel_id=1, source_target_pairs={{0,7},{1,8},{2,9},{3,10},{4,11},{5,12},{6,13},{7,14},{8,15},{9,16}... | collective-permute-start | bytes 276488
  873.9 16.0 %collective-permute-start.5 = (f32[24,960]{1,0:T(8,128)S(1)}, f32[24,960]{1,0:T(8,128)S(1)}, u32[]{:S(2)}, u32[]{:S(2)}) collective-permute-start(f32[24,960]{1,0:T(8,128)S(1)} %copy-done.43), channel_id=1, source_target_pairs={{0,6},{1,7},{2,8},{3,9},{4,10},{5,11},{6,12},{7,13},{8,14},{9,15},... | collective-permute-start | bytes 276488
  878.0 15.9 %collective-permute-start.4 = (f32[24,960]{1,0:T(8,128)S(1)}, f32[24,960]{1,0:T(8,128)S(1)}, u32[]{:S(2)}, u32[]{:S(2)}) collective-permute-start(f32[24,960]{1,0:T(8,128)S(1)} %copy-done.43), channel_id=1, source_target_pairs={{0,5},{1,6},{2,7},{3,8},{4,9},{5,10},{6,11},{7,12},{8,13},{9,14},{... | collective-permute-start | bytes 276488
  880.2 13.8 %collective-permute-start.3 = (f32[24,960]{1,0:T(8,128)S(1)}, f32[24,960]{1,0:T(8,128)S(1)}, u32[]{:S(2)}, u32[]{:S(2)}) collective-permute-start(f32[24,960]{1,0:T(8,128)S(1)} %copy-done.43), channel_id=1, source_target_pairs={{0,4},{1,5},{2,6},{3,7},{4,8},{5,9},{6,10},{7,11},{8,12},{9,13},{1... | collective-permute-start | bytes 276488
  884.5 9.5 %collective-permute-start.2 = (f32[24,960]{1,0:T(8,128)S(1)}, f32[24,960]{1,0:T(8,128)S(1)}, u32[]{:S(2)}, u32[]{:S(2)}) collective-permute-start(f32[24,960]{1,0:T(8,128)S(1)} %copy-done.43), channel_id=1, source_target_pairs={{0,3},{1,4},{2,5},{3,6},{4,7},{5,8},{6,9},{7,10},{8,11},{9,12},{10... | collective-permute-start | bytes 276488
  885.8 8.2 collective-permute-start.1
  889.9 5.5 collective-permute-start
  (95 other events, 564.0 us)
Sparse Core Ops, SparseCore 0:
  11.1 70.9 all-gather.7
  85.2 66.0 all-gather.9
  154.4 69.2 all-gather.5
  350.7 256.0 all-reduce.8
where the time goes:
time: 931 us; the launch traced here: 917 us
  blocking collectives  519 us (56%)
  matrix products  110 us (12%)
  waiting for transfers between devices  96.9 us (10%)
  local copies, waits for them, and re-layouts  90.5 us (10%)
  starting transfers between devices  68.3 us (7%)
  other arithmetic  17.3 us (2%)
  between operations  16 us (2%)
    unnamed x3, blocking collectives  519 us
    unnamed x23, starting transfers between devices  68.2 us
    all_gather x1, waiting for transfers between devices, body(): lax.all_gather(gate_up, 'dp', axis=1, tiled=True)  50.8 us
    all_gather x1, waiting for transfers between devices, body(): lax.all_gather(down_weight, 'dp', axis=0, tiled=True)  44 us
    add x1, local copies, waits for them, and re-layouts, body(): jax.tree.map(jnp.add, grad_total, grads)  35.5 us
    unnamed x208, local copies, waits for them, and re-layouts  34.8 us
    dot_general x2, matrix products, backward_pass(): jnp.einsum('crf,rd->cfd', grad_pair, normed_two, preferred_element_type=j...  22.3 us
    dot_general x2, matrix products, forward_pass(): jnp.einsum('rd,cfd->crf', normed_two, gate_full, preferred_element_type=j...  20.8 us
  transfers between devices with their start and end apart: 26, of which 2 were waited for; matrix products, arithmetic and copies ran while one was open for 51% of the time, Pallas kernels for 0%

commit v1 on v0

v1 whole, which is shorter than its diff:
```python
import jax
import jax.numpy as jnp
from jax import lax
from jax.experimental import pallas as pl
from jax.experimental.pallas import tpu as pltpu
from jax.sharding import Mesh, PartitionSpec as P

HEADS = 15
KV_HEADS = 5
GROUP = HEADS // KV_HEADS
HEAD_DIM = 64
MICRO = 2
WIDTH = 960
TOK = 128
BLOCK = 80
EPS = 1e-05
THETA = 100000.0
NEG_FILL = -1e30
AXES = ("z", "y", "x", "c")
BF = jnp.bfloat16
F32 = jnp.float32


def flat(z, y, x, c):
    return (((z % 4) * 4 + y % 4) * 4 + x % 4) * 2 + c % 2


def everywhere():
    return [(z, y, x, c) for z in range(4) for y in range(4) for x in range(4) for c in range(2)]


def shift_x(step):
    return [(flat(*d), flat(d[0], d[1], d[2] + step, d[3])) for d in everywhere()]


def shift_core():
    return [(flat(*d), flat(d[0], d[1], d[2], d[3] + 1)) for d in everywhere()]


def shift_plane(step, inner):
    pairs = []
    for z, y, x, c in everywhere():
        along_y = (c == 0) == inner
        pairs.append((flat(z, y, x, c), flat(z, y + step, x, c) if along_y else flat(z + step, y, x, c)))
    return pairs


def permute(value, pairs):
    return lax.ppermute(value, AXES, pairs)


def fetch(value, make):
    return [value] + [permute(value, make(-r)) for r in (1, 3, 2)]


def fetch_ordered(value, make):
    got = fetch(value, make)
    return [got[0], got[1], got[3], got[2]]


def place_kernel(where_ref, *refs):
    own, sib = refs[0:4], refs[4:8]
    qkv, out, gains, sem, gsem = refs[8:13]
    z, y, c = where_ref[0], where_ref[1], where_ref[2]
    gain_copies = []
    pairs = []
    for r2 in range(4):
        for r1 in range(4):
            k = r2 * 4 + r1
            for which, group in enumerate((own, sib)):
                core = c if which == 0 else 1 - c
                rz = jnp.where(core == 0, r2, r1)
                ry = jnp.where(core == 0, r1, r2)
                row = lax.rem(z + rz, 4) * 4 + lax.rem(y + ry, 4)
                source = group[r2].at[r1, pl.ds(0, BLOCK)]
                first = pltpu.make_async_copy(source, qkv.at[jnp.minimum(row, 9), core], sem.at[which, k])
                second = pltpu.make_async_copy(source, out.at[jnp.maximum(row, 10) - 10, core], sem.at[which, k])
                pairs.append((row < 10, first, second))
                if which == 0:
                    gain_copies.append(
                        pltpu.make_async_copy(
                            group[r2].at[r1, pl.ds(BLOCK, 16)], gains.at[row], gsem.at[k]
                        )
                    )
    for early, first, second in pairs:
        pl.when(early)(first.start)
        pl.when(jnp.logical_not(early))(second.start)
    for copy in gain_copies:
        copy.start()
    for early, first, second in pairs:
        pl.when(early)(first.wait)
        pl.when(jnp.logical_not(early))(second.wait)
    for copy in gain_copies:
        copy.wait()


def place(where, own, sib):
    anywhere = pl.BlockSpec(memory_space=pl.ANY)
    local = pl.BlockSpec(memory_space=pltpu.VMEM)
    return pl.pallas_call(
        place_kernel,
        in_specs=[pl.BlockSpec(memory_space=pltpu.SMEM)] + [anywhere] * 8,
        out_specs=[local] * 3,
        out_shape=[
            jax.ShapeDtypeStruct((10, 2, BLOCK, WIDTH), BF),
            jax.ShapeDtypeStruct((6, 2, BLOCK, WIDTH), BF),
            jax.ShapeDtypeStruct((16, 16, WIDTH), BF),
        ],
        scratch_shapes=[pltpu.SemaphoreType.DMA((2, 16)), pltpu.SemaphoreType.DMA((16,))],
        compiler_params=pltpu.CompilerParams(vmem_limit_bytes=8 * 2**20),
        name="place_rows",
    )(where, *own, *sib)


def attn_grads_kernel(where_ref, proj, att, normed, branch, gains, ours, theirs):
    z, y, c = where_ref[0], where_ref[1], where_ref[2]
    jobs = [(proj, 0, 640, normed), (proj, 640, 640, normed), (proj, 1280, 320, normed)]
    jobs += [(att, 0, 640, branch), (att, 640, 320, branch)]
    row = 0
    for source, start, size, right in jobs:
        block = lax.dot_general(
            source[:, start : start + size], right[...], (((0,), (0,)), ((), ())), preferred_element_type=F32
        ).astype(BF)
        for k in range(size // 160):
            rz = lax.rem(row // 4 - z + 4, 4)
            ry = lax.rem(row % 4 - y + 4, 4)
            zy, yz = rz * 4 + ry, ry * 4 + rz
            lower = block[160 * k : 160 * k + 80]
            upper = block[160 * k + 80 : 160 * k + 160]

            @pl.when(c == 0)
            def _(lower=lower, upper=upper, zy=zy, yz=yz):
                ours[zy] = lower
                theirs[yz] = upper

            @pl.when(c != 0)
            def _(lower=lower, upper=upper, zy=zy, yz=yz):
                ours[yz] = upper
                theirs[zy] = lower

            row += 1
    theirs[16] = jnp.zeros((BLOCK, WIDTH), BF)
    theirs[16, 0:16] = gains[...]


def attn_grads(where, proj, att, normed, branch, gains):
    local = pl.BlockSpec(memory_space=pltpu.VMEM)
    return pl.pallas_call(
        attn_grads_kernel,
        in_specs=[pl.BlockSpec(memory_space=pltpu.SMEM)] + [local] * 5,
        out_specs=[local] * 2,
        out_shape=[
            jax.ShapeDtypeStruct((16, BLOCK, WIDTH), BF),
            jax.ShapeDtypeStruct((17, BLOCK, WIDTH), BF),
        ],
        compiler_params=pltpu.CompilerParams(vmem_limit_bytes=12 * 2**20),
        name="attn_grads",
    )(where, proj, att, normed, branch, gains)


def ffn_kernel(count, first, normed, cot, *refs):
    chunks, refs = refs[:count], refs[count:]
    if first:
        branch, back = 0.0, 0.0
    else:
        branch, back = refs[0][...], refs[1][...]
        refs = refs[2:]
    grads, branch_out, back_out = refs[:count], refs[count], refs[count + 1]
    half = 4 * BLOCK
    for chunk, grad in zip(chunks, grads):
        pair = chunk[0:2].reshape(2 * half, WIDTH)
        down = chunk[2].reshape(half, WIDTH)
        both = dot(pair, normed[...], NT)
        grad_prod = dot(down, cot[...], NT)
        gate, up = both[:half], both[half:]
        sigma = 1.0 / (1.0 + jnp.exp(-gate))
        gated = gate * sigma
        product = (gated * up).astype(BF)
        grad_gate = (grad_prod * up * sigma * (1.0 + gate * (1.0 - sigma))).astype(BF)
        grad_up = (grad_prod * gated).astype(BF)
        grad_pair = jnp.concatenate([grad_gate, grad_up], axis=0)
        back = back + dot(grad_pair, pair, TN)
        grad[0:2] = dot(grad_pair, normed[...], NN).astype(BF).reshape(2, 4, BLOCK, WIDTH)
        grad[2] = dot(product, cot[...], NN).astype(BF).reshape(4, BLOCK, WIDTH)
        branch = branch + dot(product, down, TN)
    branch_out[...] = branch
    back_out[...] = back


def ffn(normed, cot, chunks, sums):
    local = pl.BlockSpec(memory_space=pltpu.VMEM)
    count, tokens = len(chunks), normed.shape[0]
    sums = list(sums)
    held = len(sums)
    out = pl.pallas_call(
        lambda *refs: ffn_kernel(count, held == 0, *refs),
        in_specs=[local] * (2 + count + held),
        out_specs=[local] * (count + 2),
        out_shape=[jax.ShapeDtypeStruct((3, 4, BLOCK, WIDTH), BF)] * count
        + [jax.ShapeDtypeStruct((tokens, WIDTH), F32)] * 2,
        input_output_aliases={2 + count + i: count + i for i in range(held)},
        compiler_params=pltpu.CompilerParams(vmem_limit_bytes=16 * 2**20),
        cost_estimate=pl.CostEstimate(
            flops=count * 18 * tokens * 4 * BLOCK * WIDTH,
            transcendentals=count * tokens * 4 * BLOCK,
            bytes_accessed=count * 12 * 4 * BLOCK * WIDTH,
        ),
        name="ffn_chunks",
    )(normed, cot, *chunks, *sums)
    return out[:count], out[count:]


def rope_tables(seg):
    places = jnp.arange(TOK)
    allowed = (seg[:, :, None] == seg[:, None, :]) & (places[None, :] <= places[:, None])
    position = jnp.sum(allowed.astype(F32), axis=-1) - 1.0
    freqs = THETA ** (-2.0 * jnp.arange(HEAD_DIM // 2).astype(F32) / HEAD_DIM)
    angles = position[..., None] * freqs
    return jnp.cos(angles)[:, :, None, :], jnp.sin(angles)[:, :, None, :], allowed


def rotate(values, cosine, sine):
    half = HEAD_DIM // 2
    former, latter = values[..., :half], values[..., half:]
    return jnp.concatenate([former * cosine - latter * sine, latter * cosine + former * sine], axis=-1)


def inv_rms(values):
    return lax.rsqrt(jnp.mean(values * values, axis=-1, keepdims=True) + EPS)


def norm_back(grad_normed, source, inverse, gain_vec):
    scaled = source * inverse
    grad_scaled = grad_normed * gain_vec
    grad_gain = jnp.sum(grad_normed * scaled, axis=0)
    mean = jnp.mean(grad_scaled * scaled, axis=-1, keepdims=True)
    return inverse * (grad_scaled - scaled * mean), grad_gain


def dot(left, right, dims):
    return lax.dot_general(left, right, (dims, ((), ())), preferred_element_type=F32)


NT = ((1,), (1,))
NN = ((1,), (0,))
TN = ((0,), (0,))


def total(parts):
    out = parts[0].astype(F32)
    for part in parts[1:]:
        out = out + part.astype(F32)
    return out


def body(tokens, segment_ids, attn_weight, gate_up, down_weight, norm_gains, cotangent):
    z, y, x, c = (lax.axis_index(a) for a in AXES)
    rows = MICRO * TOK
    kv_width = KV_HEADS * HEAD_DIM
    qkv_rows = WIDTH + 2 * kv_width

    gain_row = jnp.pad(norm_gains[None, :], ((0, 15), (0, WIDTH - 15)))
    shard = jnp.concatenate([attn_weight, gate_up[0], gate_up[1], down_weight, gain_row], axis=0)
    near = jnp.stack(fetch_ordered(shard, shift_x))
    ffn_block = near[:, 20:80].reshape(4, 3, 20, WIDTH).transpose(1, 0, 2, 3).reshape(3, BLOCK, WIDTH)
    head = jnp.concatenate([near[:, :20], near[:, 80:81]], axis=1)
    head = lax.dynamic_slice_in_dim(jnp.concatenate([head, head], axis=0), lax.rem(4 - x, 4), 4, axis=0)
    other = permute(head, shift_core())
    both = jnp.stack([jnp.where(c == 0, head, other), jnp.where(c == 0, other, head)], axis=1)
    attn_half = lax.dynamic_slice_in_dim(both[:, :, :20].reshape(2 * BLOCK, WIDTH), c * BLOCK, BLOCK, axis=0)
    gain_near = jnp.pad(both[:, :, 20, :15].reshape(1, 120), ((0, 15), (0, WIDTH - 120)))
    attn_block = jnp.concatenate([attn_half, gain_near], axis=0)

    block = jnp.concatenate([attn_block, ffn_block.reshape(3 * BLOCK, WIDTH)], axis=0)
    got = fetch_ordered(block, lambda s: shift_plane(s, True))
    attn_one = jnp.stack([part[:96] for part in got])
    ffn_one = jnp.stack([part[96:].reshape(3, BLOCK, WIDTH) for part in got], axis=1)
    own = fetch_ordered(attn_one, lambda s: shift_plane(s, False))
    sib = [permute(v, shift_core()) for v in own]
    where = jnp.stack([z, y, c]).astype(jnp.int32)
    w_qkv, w_out, gain_full = place(where, own, sib)
    w_qkv = w_qkv.reshape(qkv_rows, WIDTH)
    w_out = w_out.reshape(WIDTH, WIDTH)
    gain_full = gain_full[:, 0, :120].astype(F32)
    gain_attn, gain_mlp = gain_full[:8].reshape(WIDTH), gain_full[8:].reshape(WIDTH)

    ffn_send, _ = lax.optimization_barrier((ffn_one, own))
    ffn_next = permute(ffn_send, shift_plane(-1, False))
    ffn_last = permute(ffn_send, shift_plane(-3, False))
    ffn_send, ffn_next, ffn_last = lax.optimization_barrier((ffn_send, ffn_next, ffn_last))
    ffn_far = permute(ffn_send, shift_plane(-2, False))

    inputs = tokens.reshape(rows, WIDTH).astype(F32)
    live = (segment_ids.reshape(rows, 1) < TOK).astype(F32)
    grad_out = cotangent.reshape(rows, WIDTH).astype(F32)
    grad_mlp = (live * grad_out).astype(BF)
    grad_mlp_all = jnp.concatenate([grad_mlp, permute(grad_mlp, shift_core())], axis=0)
    scale_one = inv_rms(inputs)
    normed_one = (inputs * scale_one * gain_attn).astype(BF)
    projected = dot(normed_one, w_qkv, NT)
    cosine, sine, allowed = rope_tables(segment_ids)
    allowed = allowed[:, None, None]
    queries = rotate(projected[:, :WIDTH].reshape(MICRO, TOK, HEADS, HEAD_DIM), cosine, sine)
    queries = queries.astype(BF).reshape(MICRO, TOK, KV_HEADS, GROUP, HEAD_DIM)
    keys = projected[:, WIDTH : WIDTH + kv_width].reshape(MICRO, TOK, KV_HEADS, HEAD_DIM)
    keys = rotate(keys, cosine, sine).astype(BF)
    values = projected[:, WIDTH + kv_width :].reshape(MICRO, TOK, KV_HEADS, HEAD_DIM).astype(BF)
    scores = jnp.einsum("bqkgd,btkd->bkgqt", queries, keys, preferred_element_type=F32)
    scores = jnp.where(allowed, scores * HEAD_DIM ** (-0.5), NEG_FILL)
    row_max = jnp.max(scores, axis=-1, keepdims=True)
    expd = jnp.exp(scores - row_max)
    probs = expd / jnp.sum(expd, axis=-1, keepdims=True)
    probs_low = probs.astype(BF)
    attended = jnp.einsum("bkgqt,btkd->bqkgd", probs_low, values, preferred_element_type=F32)
    attended = attended.reshape(rows, WIDTH).astype(BF)
    hidden = inputs + live * dot(attended, w_out, NN)

    scale_two = inv_rms(hidden)
    normed_two = (hidden * scale_two * gain_mlp).astype(BF)
    normed_all = jnp.concatenate([normed_two, permute(normed_two, shift_core())], axis=0)
    (grad_zero,), sums = ffn(normed_all, grad_mlp_all, [ffn_one], [])
    (grad_next, grad_last), sums = ffn(normed_all, grad_mlp_all, [ffn_next, ffn_last], sums)
    (grad_far,), (branch, grad_normed) = ffn(normed_all, grad_mlp_all, [ffn_far], sums)
    grad_normed = grad_normed[:rows] + permute(grad_normed[rows:].astype(BF), shift_core()).astype(F32)
    branch = branch[:rows] + permute(branch[rows:].astype(BF), shift_core()).astype(F32)
    result = (hidden + live * branch).astype(BF)

    got = [
        grad_zero,
        permute(grad_next, shift_plane(1, False)),
        permute(grad_last, shift_plane(3, False)),
        permute(grad_far, shift_plane(2, False)),
    ]
    mine = total(got).astype(BF)
    got = [mine[:, 0]] + [permute(mine[:, r], shift_plane(r, True)) for r in (1, 3, 2)]
    mine = total(got).astype(BF).reshape(3, 4, 20, WIDTH)
    got = [mine[:, 0]] + [permute(mine[:, r], shift_x(r)) for r in (1, 3, 2)]
    ffn_owned = total(got)

    grad_hidden, grad_gain_mlp = norm_back(grad_normed, hidden, scale_two, gain_mlp)
    grad_hidden = grad_out + grad_hidden
    grad_branch = (live * grad_hidden).astype(BF)
    grad_att = dot(grad_branch, w_out, NT).astype(BF)
    grad_att = grad_att.reshape(MICRO, TOK, KV_HEADS, GROUP, HEAD_DIM)
    grad_probs = jnp.einsum("bqkgd,btkd->bkgqt", grad_att, values, preferred_element_type=F32)
    delta = jnp.sum(probs * grad_probs, axis=-1, keepdims=True)
    grad_scores = (HEAD_DIM ** (-0.5) * probs * (grad_probs - delta)).astype(BF)
    grad_q = jnp.einsum("bkgqt,btkd->bqkgd", grad_scores, keys, preferred_element_type=F32)
    grad_k = jnp.einsum("bkgqt,bqkgd->btkd", grad_scores, queries, preferred_element_type=F32)
    grad_v = jnp.einsum("bkgqt,bqkgd->btkd", probs_low, grad_att, preferred_element_type=F32)
    grad_q = rotate(grad_q.reshape(MICRO, TOK, HEADS, HEAD_DIM), cosine, -sine)
    grad_k = rotate(grad_k, cosine, -sine)
    grad_proj = jnp.concatenate(
        [grad_q.reshape(rows, WIDTH), grad_k.reshape(rows, kv_width), grad_v.reshape(rows, kv_width)], axis=1
    ).astype(BF)
    grad_normed_one = dot(grad_proj, w_qkv, NN)
    grad_inputs, grad_gain_attn = norm_back(grad_normed_one, inputs, scale_one, gain_attn)
    grad_inputs = (grad_hidden + grad_inputs).astype(BF)

    def spread(value):
        return jnp.pad(value.astype(BF), ((0, 14), (0, 0)))

    gain_grads = jnp.stack([grad_gain_attn, grad_gain_mlp])
    ours, theirs = attn_grads(where, grad_proj, attended, normed_one, grad_branch, spread(gain_grads))
    swapped = permute(theirs, shift_core())
    mine = total([ours, swapped[:16]]).astype(BF).reshape(4, 4 * BLOCK, WIDTH)
    gain_grads = gain_grads + swapped[16, :2].astype(F32)

    def exchange(blocks, gain_grads, make):
        count = blocks.shape[1]
        low = spread(gain_grads)
        got = [
            permute(jnp.concatenate([blocks[r], low], axis=0), make(r)) for r in (1, 3, 2)
        ]
        blocks = total([blocks[0]] + [part[:count] for part in got])
        return blocks, total([gain_grads] + [part[count : count + 2] for part in got])

    mine, gain_grads = exchange(mine, gain_grads, lambda r: shift_plane(r, False))
    mine = mine.astype(BF).reshape(4, BLOCK, WIDTH)
    mine, gain_grads = exchange(mine, gain_grads, lambda r: shift_plane(r, True))
    mine = mine.astype(BF).reshape(2, 2, 20, WIDTH)
    keep = lax.dynamic_index_in_dim(mine, c, 1, keepdims=False)
    give = lax.dynamic_index_in_dim(mine, 1 - c, 1, keepdims=False)
    take = permute(give, shift_core())
    mine = jnp.concatenate([jnp.where(c == 0, keep, take), jnp.where(c == 0, take, keep)], axis=0)
    mine = lax.dynamic_slice_in_dim(jnp.concatenate([mine, mine], axis=0), x, 4, axis=0)
    attn_owned, gain_grads = exchange(mine, gain_grads, shift_x)
    gain_owned = lax.dynamic_slice_in_dim(gain_grads.reshape(2 * WIDTH), flat_index(z, y, x, c) * 15, 15)
    return (
        result.reshape(MICRO, TOK, WIDTH),
        grad_inputs.reshape(MICRO, TOK, WIDTH),
        attn_owned,
        ffn_owned[:2],
        ffn_owned[2],
        gain_owned,
    )


def flat_index(z, y, x, c):
    return ((z * 4 + y) * 4 + x) * 2 + c


def solution(mesh):
    grid = Mesh(mesh.devices.reshape(4, 4, 4, 2), AXES)
    return jax.shard_map(
        body,
        mesh=grid,
        in_specs=(
            P(None, AXES, None),
            P(None, AXES),
            P(AXES, None),
            P(None, AXES, None),
            P(AXES, None),
            P(AXES),
            P(None, AXES, None),
        ),
        out_specs=(
            P(None, AXES, None),
            P(None, AXES, None),
            P(AXES, None),
            P(None, AXES, None),
            P(AXES, None),
            P(AXES),
        ),
        check_vma=False,
    )
```

time: 931 us -> 270 us (0.29); the launches traced: 917 us -> 267 us
  blocking collectives: 519 us -> 0 us
  matrix products: 110 us -> 17.6 us
  local copies, waits for them, and re-layouts: 90.5 us -> 36.1 us
  Pallas kernels: 0 us -> 44.6 us
  starting transfers between devices: 68.3 us -> 50.8 us
  other arithmetic: 17.3 us -> 33.4 us
  waiting for transfers between devices: 96.9 us -> 82.8 us
  between operations: 16 us -> 2.07 us
    unnamed x3 -> x0, blocking collectives: 519 us -> none
    dot_general x36 -> x9, matrix products: 110 us -> 14.8 us  [the longest x4 11 us: dot(): lax.dot_general(left, right, (dims, ((), ())), preferred_element_type=F32)]
    all_gather x3 -> x0, waiting for transfers between devices: 94.8 us -> none  [the longest x1 50.8 us: body(): lax.all_gather(gate_up, 'dp', axis=1, tiled=True)]
    ppermute x0 -> x41, waiting for transfers between devices: none -> 82.8 us  [permute(): return lax.ppermute(value, AXES, pairs)]
    unnamed x23 -> x0, starting transfers between devices: 68.2 us -> none
    ppermute x0 -> x41, starting transfers between devices: none -> 50.8 us  [permute(): return lax.ppermute(value, AXES, pairs)]
    pallas_call x0 -> x5, Pallas kernels: none -> 44.6 us  [the longest x3 20.3 us: ffn(): pl.pallas_call(lambda *refs: ffn_kernel(count, held == 0, *refs), in_spec...]
    add x1 -> x0, local copies, waits for them, and re-layouts: 35.5 us -> none  [body(): jax.tree.map(jnp.add, grad_total, grads)]
  transfers between devices with their start and end apart: 26 -> 41, of which waited for: 2 -> 20; matrix products, arithmetic and copies ran while one was open for 51% -> 26% of each run, Pallas kernels for 0% -> 15%
where the time goes in v1:
time: 270 us; the launch traced here: 267 us
  waiting for transfers between devices  82.8 us (31%)
  starting transfers between devices  50.8 us (19%)
  Pallas kernels  44.6 us (17%)
  local copies, waits for them, and re-layouts  36.1 us (13%)
  other arithmetic  33.4 us (12%)
  matrix products  17.6 us (7%)
    ppermute x41, waiting for transfers between devices, permute(): return lax.ppermute(value, AXES, pairs)  82.8 us
    ppermute x41, starting transfers between devices, permute(): return lax.ppermute(value, AXES, pairs)  50.8 us
    pallas_call x3, Pallas kernels, ffn(): pl.pallas_call(lambda *refs: ffn_kernel(count, held == 0, *refs), in_spec...  20.3 us
    pallas_call x1, Pallas kernels, place(): pl.pallas_call(place_kernel, in_specs=[pl.BlockSpec(memory_space=pltpu.SM...  19.2 us
    unnamed x125, local copies, waits for them, and re-layouts  13.8 us
    dot_general x4, matrix products, dot(): lax.dot_general(left, right, (dims, ((), ())), preferred_element_type=F32)  11 us
  transfers between devices with their start and end apart: 41, of which 20 were waited for; matrix products, arithmetic and copies ran while one was open for 26% of the time, Pallas kernels for 15%

profile of v1, /device:TPU:0, one launch (start us, length us, event | category | flops | bytes accessed | tf_op | source)
XLA Modules:
  0.0 267.4 jit_solution(84927692231177409)
XLA Ops:
  6.0 2.7 %collective-permute-start.1 = (bf16[96,960]{1,0:T(8,128)(2,1)S(1)}, bf16[96,960]{1,0:T(8,128)(2,1)S(1)}, u32[]{:S(2)}, u32[]{:S(2)}) collective-permute-start(bf16[96,960]{1,0:T(8,128)(2,1)S(1)} %concatenate.79), channel_id=1, source_target_pairs={{0,4},{1,5},{2,6},{3,7},{4,0},{5,1},{6,2},{7,3},{8,12},{9,13},{10,... | collective-permute-start | bytes 552968 | tf_op jit(solution)/shard_map/ppermute | solution.py:49
  12.1 5.4 %collective-permute-done.1 = bf16[96,960]{1,0:T(8,128)(2,1)S(1)} collective-permute-done((bf16[96,960]{1,0:T(8,128)(2,1)S(1)}, bf16[96,960]{1,0:T(8,128)(2,1)S(1)}, u32[]{:S(2)}, u32[]{:S(2)}) %collective-permute-start.1) | collective-permute-done | bytes 184352 | tf_op jit(solution)/shard_map/ppermute | solution.py:49
  21.8 2.9 %collective-permute-start.5 = (bf16[336,960]{1,0:T(8,128)(2,1)S(1)}, bf16[336,960]{1,0:T(8,128)(2,1)S(1)}, u32[]{:S(2)}, u32[]{:S(2)}) collective-permute-start(bf16[336,960]{1,0:T(8,128)(2,1)S(1)} %pad_maximum_fusion.4), channel_id=1, source_target_pairs={{0,16},{1,65},{2,18},{3,67},{4,20},{5,69},{6,22},{7,71},{8,24},{9,... | collective-permute-start | bytes 1935368 | tf_op jit(solution)/shard_map/ppermute | solution.py:49
  26.3 3.0 %collective-permute-start.4 = (bf16[336,960]{1,0:T(8,128)(2,1)S(1)}, bf16[336,960]{1,0:T(8,128)(2,1)S(1)}, u32[]{:S(2)}, u32[]{:S(2)}) collective-permute-start(bf16[336,960]{1,0:T(8,128)(2,1)S(1)} %pad_maximum_fusion.4), channel_id=1, source_target_pairs={{0,24},{1,97},{2,26},{3,99},{4,28},{5,101},{6,30},{7,103},{8,0},{9... | collective-permute-start | bytes 1935368 | tf_op jit(solution)/shard_map/ppermute | solution.py:49
  29.3 3.0 %collective-permute-done.6 = bf16[336,960]{1,0:T(8,128)(2,1)S(1)} collective-permute-done((bf16[336,960]{1,0:T(8,128)(2,1)S(1)}, bf16[336,960]{1,0:T(8,128)(2,1)S(1)}, u32[]{:S(2)}, u32[]{:S(2)}) %collective-permute-start.6) | collective-permute-done | bytes 645152 | tf_op jit(solution)/shard_map/ppermute | solution.py:49
  32.3 8.6 %collective-permute-done.5 = bf16[336,960]{1,0:T(8,128)(2,1)S(1)} collective-permute-done((bf16[336,960]{1,0:T(8,128)(2,1)S(1)}, bf16[336,960]{1,0:T(8,128)(2,1)S(1)}, u32[]{:S(2)}, u32[]{:S(2)}) %collective-permute-start.5) | collective-permute-done | bytes 645152 | tf_op jit(solution)/shard_map/ppermute | solution.py:49
  42.0 4.1 %collective-permute-start.7 = (bf16[4,96,960]{2,1,0:T(8,128)(2,1)S(1)}, bf16[4,96,960]{2,1,0:T(8,128)(2,1)S(1)}, u32[]{:S(2)}, u32[]{:S(2)}) collective-permute-start(bf16[4,96,960]{2,1,0:T(8,128)(2,1)S(1)} %pad_maximum_fusion.3.refs_0_), channel_id=1, source_target_pairs={{0,96},{1,25},{2,98},{3,27},{4,100},{5,29},{6,102},{7,31},{8,104},... | collective-permute-start | bytes 2211848 | tf_op jit(solution)/shard_map/ppermute | solution.py:49
  47.4 2.2 copy.61
  53.7 10.4 %collective-permute-done.7.refs_1_ = bf16[4,96,960]{2,1,0:T(8,128)(2,1)S(1)} collective-permute-done((bf16[4,96,960]{2,1,0:T(8,128)(2,1)S(1)}, bf16[4,96,960]{2,1,0:T(8,128)(2,1)S(1)}, u32[]{:S(2)}, u32[]{:S(2)}) %collective-permute-start.7) | collective-permute-done | bytes 737312 | tf_op jit(solution)/shard_map/ppermute | solution.py:49
  64.6 3.3 %collective-permute-done.9.refs_3_ = bf16[4,96,960]{2,1,0:T(8,128)(2,1)S(1)} collective-permute-done((bf16[4,96,960]{2,1,0:T(8,128)(2,1)S(1)}, bf16[4,96,960]{2,1,0:T(8,128)(2,1)S(1)}, u32[]{:S(2)}, u32[]{:S(2)}) %collective-permute-start.9) | collective-permute-done | bytes 737312 | tf_op jit(solution)/shard_map/ppermute | solution.py:49
  76.4 19.2 %place_rows.1 = (bf16[10,2,80,960]{3,2,1,0:T(8,128)(2,1)S(1)}, bf16[6,2,80,960]{3,2,1,0:T(8,128)(2,1)S(1)}, bf16[16,16,960]{2,1,0:T(8,128)(2,1)S(1)}) custom-call(s32[3]{0:T(128)S(1)} %pad_add_fusion.where_ref, bf16[4,96,960]{2,1,0:T(8,128)(2,1)S(1)} %pad_maximum_fusion.3.refs_0_, bf16[4,96,960]{2,1,0:T(8,128)(2,1)S(1)} %collective-permute-done.7.refs_1_, ...), custom_call_target="tpu_custom_call" | custom-call | tf_op jit(solution)/shard_map/place_rows/pallas_call | solution.py:100
  97.5 3.8 %fusion.24 = f32[256,1600]{0,1:T(8,128)S(1)} fusion(bf16[1600,960]{1,0:T(8,128)(2,1)} %bitcast.232, bf16[2,128,960]{1,2,0:T(8,128)(2,1)} %param.7, f32[960]{0:T(1024)S(1)} %mul.308, f32[2,128]{1,0:T(2,128)} %get-tuple-element.117), kind=kOutput, calls=%fused_computation.67 | convolution fusion | flops 787415040 | bytes 5206784 | tf_op jit(solution)/shard_map/dot_general | solution.py:241
  106.8 2.9 %fusion.73 = (f32[2,5,3,128]{3,2,1,0:T(4,128)S(1)}, f32[2,5,3,128,128]{3,4,2,1,0:T(8,128)}) fusion(pred[2,128,128]{1,2,0:T(8,128)(4,1)} %compare_and_fusion, bf16[2,128,5,3,32]{1,4,3,2,0:T(8,128)(2,1)S(1)} %bitcast.263, bf16[2,128,5,3,32]{1,4,3,2,0:T(8,128)(2,1)S(1)} %bitcast.265, bf16[2,128,5,32]{1,3,2,0:T(8,128)(2,1)S(1)} %get-tuple-element.92, ...), kind=kOutput, calls=%fused_computation.194 | convolution fusion | flops 66191488 | bytes 2669568 | tf_op jit(solution)/shard_map/sub | solution.py:311
  112.2 2.2 multiply_reduce_fusion.4
  118.7 5.5 %ffn_chunks.3 = (bf16[3,4,80,960]{3,2,1,0:T(8,128)(2,1)S(1)}, f32[512,960]{1,0:T(8,128)S(1)}, f32[512,960]{1,0:T(8,128)S(1)}) custom-call(bf16[512,960]{1,0:T(8,128)(2,1)S(1)} %pad_maximum_fusion.1.refs_0_, bf16[512,960]{1,0:T(8,128)(2,1)S(1)} %pad_maximum_fusion.2.refs_1_, bf16[3,4,80,960]{3,2,1,0:T(8,128)(2,1)} %pad_maximum_fusion.refs_2_), custom_call_target="tpu_custom_call" | custom-call | flops 2831155200 | bytes 3686400 | tf_op jit(solution)/shard_map/ffn_chunks/pallas_call | solution.py:195
  125.5 10.3 %ffn_chunks.4 = (bf16[3,4,80,960]{3,2,1,0:T(8,128)(2,1)S(1)}, bf16[3,4,80,960]{3,2,1,0:T(8,128)(2,1)S(1)}, f32[512,960]{1,0:T(8,128)S(1)}, f32[512,960]{1,0:T(8,128)S(1)}) custom-call(bf16[512,960]{1,0:T(8,128)(2,1)S(1)} %pad_maximum_fusion.1.refs_0_, bf16[512,960]{1,0:T(8,128)(2,1)S(1)} %pad_maximum_fusion.2.refs_1_, ...), custom_call_target="tpu_custom_call", output_to_operand_aliasing={{2}: (4, {}), {3}: (5, {})} | custom-call | flops 5662310400 | bytes 7372800 | tf_op jit(solution)/shard_map/ffn_chunks/pallas_call | solution.py:195
  135.9 4.9 %collective-permute-done.18.refs_2_ = bf16[3,4,80,960]{3,2,1,0:T(8,128)(2,1)S(1)} collective-permute-done((bf16[3,4,80,960]{3,2,1,0:T(8,128)(2,1)}, bf16[3,4,80,960]{3,2,1,0:T(8,128)(2,1)S(1)}, u32[]{:S(2)}, u32[]{:S(2)}) %collective-permute-start.18) | collective-permute-done | bytes 1843232 | tf_op jit(solution)/shard_map/ppermute | solution.py:49
  140.8 4.5 %ffn_chunks.5 = (bf16[3,4,80,960]{3,2,1,0:T(8,128)(2,1)S(1)}, f32[512,960]{1,0:T(8,128)S(1)}, f32[512,960]{1,0:T(8,128)S(1)}) custom-call(bf16[512,960]{1,0:T(8,128)(2,1)S(1)} %pad_maximum_fusion.1.refs_0_, bf16[512,960]{1,0:T(8,128)(2,1)S(1)} %pad_maximum_fusion.2.refs_1_, ...), custom_call_target="tpu_custom_call", output_to_operand_aliasing={{1}: (3, {}), {2}: (4, {})} | custom-call | flops 2831155200 | bytes 3686400 | tf_op jit(solution)/shard_map/ffn_chunks/pallas_call | solution.py:195
  155.7 3.3 %multiply_convert_fusion.1 = (bf16[256,960]{1,0:T(8,128)(2,1)S(1)}, f32[256,960]{1,0:T(8,128)}, bf16[256,960]{1,0:T(8,128)(2,1)}) fusion(f32[256]{0:T(256)S(1)} %fusion.56, f32[256]{0:T(256)S(1)} %broadcast_multiply_fusion.1, f32[256,960]{1,0:T(8,128)S(1)} %copy-done.17, f32[960]{0:T(1024)S(1)} %mul.332, bf16[256,960]{1,0:T(8,128)(2,1)} %collective-permute-done.20, ...), kind=kLoop, calls=%fused_computation.40 | loop fusion | flops 3686400 | bytes 6888192 | tf_op jit(solution)/shard_map/convert_element_type | solution.py:342
  168.3 4.3 %multiply_reduce_fusion.1 = (f32[960]{0:T(1024)S(1)}, f32[256]{0:T(256)S(1)}, bf16[256,960]{1,0:T(8,128)(2,1)S(1)}, f32[256,960]{1,0:T(8,128)}) fusion(f32[2,128,960]{2,1,0:T(8,128)S(1)} %copy-done.19, f32[256]{0:T(256)S(1)} %copy-done.58, f32[960]{0:T(1024)S(1)} %mul.308, bf16[256,1600]{1,0:T(8,128)(2,1)S(1)} %concatenate.92.proj, ...), kind=kOutput, calls=%fused_computation.36 | convolution fusion | flops 788396864 | bytes 6358528 | tf_op jit(solution)/shard_map/dot_general | solution.py:241
  172.6 5.1 %attn_grads.1 = (bf16[16,80,960]{2,1,0:T(8,128)(2,1)S(1)}, bf16[17,80,960]{2,1,0:T(8,128)(2,1)}) custom-call(s32[3]{0:T(128)S(1)} %pad_add_fusion.where_ref, bf16[256,1600]{1,0:T(8,128)(2,1)S(1)} %concatenate.92.proj, bf16[256,960]{1,0:T(8,128)(2,1)S(1)} %copy-done, bf16[256,960]{1,0:T(8,128)(2,1)S(1)} %get-tuple-element.75.normed, ...), custom_call_target="tpu_custom_call" | custom-call | tf_op jit(solution)/shard_map/attn_grads/pallas_call | solution.py:148
  178.7 17.6 %collective-permute-done.33 = bf16[3,4,80,960]{3,2,1,0:T(8,128)(2,1)} collective-permute-done((bf16[3,4,80,960]{3,2,1,0:T(8,128)(2,1)}, bf16[3,4,80,960]{3,2,1,0:T(8,128)(2,1)}, u32[]{:S(2)}, u32[]{:S(2)}) %collective-permute-start.33) | collective-permute-done | bytes 1843232 | tf_op jit(solution)/shard_map/ppermute | solution.py:49
  196.2 3.7 %collective-permute-done.32 = bf16[3,4,80,960]{3,2,1,0:T(8,128)(2,1)} collective-permute-done((bf16[3,4,80,960]{3,2,1,0:T(8,128)(2,1)}, bf16[3,4,80,960]{3,2,1,0:T(8,128)(2,1)}, u32[]{:S(2)}, u32[]{:S(2)}) %collective-permute-start.32) | collective-permute-done | bytes 1843232 | tf_op jit(solution)/shard_map/ppermute | solution.py:49
  199.9 5.2 %add_convert_fusion.1 = bf16[3,4,80,960]{3,2,1,0:T(8,128)(2,1)S(1)} fusion(bf16[3,4,80,960]{3,2,1,0:T(8,128)(2,1)} %collective-permute-done.34, bf16[3,4,80,960]{3,2,1,0:T(8,128)(2,1)} %collective-permute-done.33, bf16[3,4,80,960]{3,2,1,0:T(8,128)(2,1)} %collective-permute-done.32, bf16[3,4,80,960]{3,2,1,0:T(8,128)(2,1)} %copy-done.3), kind=kLoop, calls=%fused_computation.2 | loop fusion | flops 7372800 | bytes 9216000 | tf_op jit(solution)/shard_map/convert_element_type | solution.py:334
  206.3 2.8 %collective-permute-start.37 = (bf16[3,80,960]{2,1,0:T(8,128)(2,1)S(1)}, bf16[3,80,960]{2,1,0:T(8,128)(2,1)S(1)}, u32[]{:S(2)}, u32[]{:S(2)}) collective-permute-start(bf16[3,80,960]{2,1,0:T(8,128)(2,1)S(1)} %get-tuple-element.73), channel_id=1, source_target_pairs={{0,16},{1,65},{2,18},{3,67},{4,20},{5,69},{6,22},{7,71},{8,24},{9,... | collective-permute-start | bytes 1382408 | tf_op jit(solution)/shard_map/ppermute | solution.py:49
  211.8 3.0 %add_convert_fusion = bf16[16,80,960]{2,1,0:T(8,128)(2,1)S(1)} fusion(bf16[16,80,960]{2,1,0:T(8,128)(2,1)S(1)} %get-tuple-element.38, bf16[17,80,960]{2,1,0:T(8,128)(2,1)} %collective-permute-done.21), kind=kLoop, calls=%fused_computation.1 | loop fusion | flops 4915200 | bytes 7372800 | tf_op jit(solution)/shard_map/convert_element_type | solution.py:366
  220.9 12.2 %collective-permute-done.36 = bf16[3,80,960]{2,1,0:T(8,128)(2,1)} collective-permute-done((bf16[3,80,960]{2,1,0:T(8,128)(2,1)}, bf16[3,80,960]{2,1,0:T(8,128)(2,1)}, u32[]{:S(2)}, u32[]{:S(2)}) %collective-permute-start.36) | collective-permute-done | bytes 460832 | tf_op jit(solution)/shard_map/ppermute | solution.py:49
  235.0 2.7 %collective-permute-start.40 = (bf16[3,20,960]{2,1,0:T(8,128)(2,1)S(1)}, bf16[3,20,960]{2,1,0:T(8,128)(2,1)S(1)}, u32[]{:S(2)}, u32[]{:S(2)}) collective-permute-start(bf16[3,20,960]{2,1,0:T(8,128)(2,1)S(1)} %get-tuple-element.87), channel_id=1, source_target_pairs={{0,4},{1,5},{2,6},{3,7},{4,0},{5,1},{6,2},{7,3},{8,12},{9,13},{10,... | collective-permute-start | bytes 345608 | tf_op jit(solution)/shard_map/ppermute | solution.py:49
  242.7 4.3 %collective-permute-start.27 = (bf16[96,960]{1,0:T(8,128)(2,1)S(1)}, bf16[96,960]{1,0:T(8,128)(2,1)S(1)}, u32[]{:S(2)}, u32[]{:S(2)}) collective-permute-start(bf16[96,960]{1,0:T(8,128)(2,1)S(1)} %get-tuple-element.109), channel_id=1, source_target_pairs={{0,16},{1,65},{2,18},{3,67},{4,20},{5,69},{6,22},{7,71},{8,24},{9,... | collective-permute-start | bytes 552968 | tf_op jit(solution)/shard_map/ppermute | solution.py:49
  250.6 2.4 collective-permute-done.26
  253.1 2.1 collective-permute-done.25
  257.9 2.3 collective-permute-start.30
  (312 shorter events, 95.6 us)
Async XLA Ops:
  6.0 11.6 %collective-permute-start.1 = (bf16[96,960]{1,0:T(8,128)(2,1)S(1)}, bf16[96,960]{1,0:T(8,128)(2,1)S(1)}, u32[]{:S(2)}, u32[]{:S(2)}) collective-permute-start(bf16[96,960]{1,0:T(8,128)(2,1)S(1)} %concatenate.79), channel_id=1, source_target_pairs={{0,4},{1,5},{2,6},{3,7},{4,0},{5,1},{6,2},{7,3},{8,12},{9,13},{10,... | collective-permute-start | bytes 552968 | tf_op jit(solution)/shard_map/ppermute | solution.py:49
  8.7 8.8 %collective-permute-start = (bf16[96,960]{1,0:T(8,128)(2,1)S(1)}, bf16[96,960]{1,0:T(8,128)(2,1)S(1)}, u32[]{:S(2)}, u32[]{:S(2)}) collective-permute-start(bf16[96,960]{1,0:T(8,128)(2,1)S(1)} %concatenate.79), channel_id=1, source_target_pairs={{0,6},{1,7},{2,0},{3,1},{4,2},{5,3},{6,4},{7,5},{8,14},{9,15},{10,... | collective-permute-start | bytes 552968 | tf_op jit(solution)/shard_map/ppermute | solution.py:49
  20.1 12.2 %collective-permute-start.6 = (bf16[336,960]{1,0:T(8,128)(2,1)S(1)}, bf16[336,960]{1,0:T(8,128)(2,1)S(1)}, u32[]{:S(2)}, u32[]{:S(2)}) collective-permute-start(bf16[336,960]{1,0:T(8,128)(2,1)S(1)} %pad_maximum_fusion.4), channel_id=1, source_target_pairs={{0,8},{1,33},{2,10},{3,35},{4,12},{5,37},{6,14},{7,39},{8,16},{9,4... | collective-permute-start | bytes 1935368 | tf_op jit(solution)/shard_map/ppermute | solution.py:49
  21.8 19.2 %collective-permute-start.5 = (bf16[336,960]{1,0:T(8,128)(2,1)S(1)}, bf16[336,960]{1,0:T(8,128)(2,1)S(1)}, u32[]{:S(2)}, u32[]{:S(2)}) collective-permute-start(bf16[336,960]{1,0:T(8,128)(2,1)S(1)} %pad_maximum_fusion.4), channel_id=1, source_target_pairs={{0,16},{1,65},{2,18},{3,67},{4,20},{5,69},{6,22},{7,71},{8,24},{9,... | collective-permute-start | bytes 1935368 | tf_op jit(solution)/shard_map/ppermute | solution.py:49
  25.6 91.5 %collective-permute-start.15 = (bf16[256,960]{1,0:T(8,128)(2,1)}, bf16[256,960]{1,0:T(8,128)(2,1)}, u32[]{:S(2)}, u32[]{:S(2)}) collective-permute-start(bf16[256,960]{1,0:T(8,128)(2,1)} %fusion.13), channel_id=1, source_target_pairs={{0,1},{1,0},{2,3},{3,2},{4,5},{5,4},{6,7},{7,6},{8,9},{9,8},{10,11... | collective-permute-start | bytes 1474568 | tf_op jit(solution)/shard_map/ppermute | solution.py:49
  26.3 14.7 %collective-permute-start.4 = (bf16[336,960]{1,0:T(8,128)(2,1)S(1)}, bf16[336,960]{1,0:T(8,128)(2,1)S(1)}, u32[]{:S(2)}, u32[]{:S(2)}) collective-permute-start(bf16[336,960]{1,0:T(8,128)(2,1)S(1)} %pad_maximum_fusion.4), channel_id=1, source_target_pairs={{0,24},{1,97},{2,26},{3,99},{4,28},{5,101},{6,30},{7,103},{8,0},{9... | collective-permute-start | bytes 1935368 | tf_op jit(solution)/shard_map/ppermute | solution.py:49
  42.0 22.0 %collective-permute-start.7 = (bf16[4,96,960]{2,1,0:T(8,128)(2,1)S(1)}, bf16[4,96,960]{2,1,0:T(8,128)(2,1)S(1)}, u32[]{:S(2)}, u32[]{:S(2)}) collective-permute-start(bf16[4,96,960]{2,1,0:T(8,128)(2,1)S(1)} %pad_maximum_fusion.3.refs_0_), channel_id=1, source_target_pairs={{0,96},{1,25},{2,98},{3,27},{4,100},{5,29},{6,102},{7,31},{8,104},... | collective-permute-start | bytes 2211848 | tf_op jit(solution)/shard_map/ppermute | solution.py:49
  46.1 17.9 %collective-permute-start.8 = (bf16[4,96,960]{2,1,0:T(8,128)(2,1)S(1)}, bf16[4,96,960]{2,1,0:T(8,128)(2,1)S(1)}, u32[]{:S(2)}, u32[]{:S(2)}) collective-permute-start(bf16[4,96,960]{2,1,0:T(8,128)(2,1)S(1)} %pad_maximum_fusion.3.refs_0_), channel_id=1, source_target_pairs={{0,64},{1,17},{2,66},{3,19},{4,68},{5,21},{6,70},{7,23},{8,72},{9,... | collective-permute-start | bytes 2211848 | tf_op jit(solution)/shard_map/ppermute | solution.py:49
  46.1 21.7 %collective-permute-start.9 = (bf16[4,96,960]{2,1,0:T(8,128)(2,1)S(1)}, bf16[4,96,960]{2,1,0:T(8,128)(2,1)S(1)}, u32[]{:S(2)}, u32[]{:S(2)}) collective-permute-start(bf16[4,96,960]{2,1,0:T(8,128)(2,1)S(1)} %pad_maximum_fusion.3.refs_0_), channel_id=1, source_target_pairs={{0,32},{1,9},{2,34},{3,11},{4,36},{5,13},{6,38},{7,15},{8,40},{9,1... | collective-permute-start | bytes 2211848 | tf_op jit(solution)/shard_map/ppermute | solution.py:49
  53.6 20.8 %collective-permute-start.10 = (bf16[4,96,960]{2,1,0:T(8,128)(2,1)S(1)}, bf16[4,96,960]{2,1,0:T(8,128)(2,1)}, u32[]{:S(2)}, u32[]{:S(2)}) collective-permute-start(bf16[4,96,960]{2,1,0:T(8,128)(2,1)S(1)} %pad_maximum_fusion.3.refs_0_), channel_id=1, source_target_pairs={{0,1},{1,0},{2,3},{3,2},{4,5},{5,4},{6,7},{7,6},{8,9},{9,8},{10,11... | collective-permute-start | bytes 2211848 | tf_op jit(solution)/shard_map/ppermute | solution.py:49
  64.0 11.2 %collective-permute-start.11 = (bf16[4,96,960]{2,1,0:T(8,128)(2,1)S(1)}, bf16[4,96,960]{2,1,0:T(8,128)(2,1)}, u32[]{:S(2)}, u32[]{:S(2)}) collective-permute-start(bf16[4,96,960]{2,1,0:T(8,128)(2,1)S(1)} %collective-permute-done.7.refs_1_), channel_id=1, source_target_pairs={{0,1},{1,0},{2,3},{3,2},{4,5},{5,4},{6,7},{7,6},{8,9},{9,8},{10,11... | collective-permute-start | bytes 2211848 | tf_op jit(solution)/shard_map/ppermute | solution.py:49
  64.1 12.4 %collective-permute-start.12 = (bf16[4,96,960]{2,1,0:T(8,128)(2,1)S(1)}, bf16[4,96,960]{2,1,0:T(8,128)(2,1)}, u32[]{:S(2)}, u32[]{:S(2)}) collective-permute-start(bf16[4,96,960]{2,1,0:T(8,128)(2,1)S(1)} %collective-permute-done.8.refs_2_), channel_id=1, source_target_pairs={{0,1},{1,0},{2,3},{3,2},{4,5},{5,4},{6,7},{7,6},{8,9},{9,8},{10,11... | collective-permute-start | bytes 2211848 | tf_op jit(solution)/shard_map/ppermute | solution.py:49
  67.8 8.6 %collective-permute-start.13 = (bf16[4,96,960]{2,1,0:T(8,128)(2,1)S(1)}, bf16[4,96,960]{2,1,0:T(8,128)(2,1)}, u32[]{:S(2)}, u32[]{:S(2)}) collective-permute-start(bf16[4,96,960]{2,1,0:T(8,128)(2,1)S(1)} %collective-permute-done.9.refs_3_), channel_id=1, source_target_pairs={{0,1},{1,0},{2,3},{3,2},{4,5},{5,4},{6,7},{7,6},{8,9},{9,8},{10,11... | collective-permute-start | bytes 2211848 | tf_op jit(solution)/shard_map/ppermute | solution.py:49
  74.4 40.0 %collective-permute-start.16 = (bf16[3,4,80,960]{3,2,1,0:T(8,128)(2,1)}, bf16[3,4,80,960]{3,2,1,0:T(8,128)(2,1)}, u32[]{:S(2)}, u32[]{:S(2)}) collective-permute-start(bf16[3,4,80,960]{3,2,1,0:T(8,128)(2,1)} %pad_maximum_fusion.refs_2_), channel_id=1, source_target_pairs={{0,96},{1,25},{2,98},{3,27},{4,100},{5,29},{6,102},{7,31},{8,104},... | collective-permute-start | bytes 5529608 | tf_op jit(solution)/shard_map/ppermute | solution.py:49
  75.2 39.1 %collective-permute-start.17 = (bf16[3,4,80,960]{3,2,1,0:T(8,128)(2,1)}, bf16[3,4,80,960]{3,2,1,0:T(8,128)(2,1)}, u32[]{:S(2)}, u32[]{:S(2)}) collective-permute-start(bf16[3,4,80,960]{3,2,1,0:T(8,128)(2,1)} %pad_maximum_fusion.refs_2_), channel_id=1, source_target_pairs={{0,32},{1,9},{2,34},{3,11},{4,36},{5,13},{6,38},{7,15},{8,40},{9,1... | collective-permute-start | bytes 5529608 | tf_op jit(solution)/shard_map/ppermute | solution.py:49
  114.4 26.4 %collective-permute-start.18 = (bf16[3,4,80,960]{3,2,1,0:T(8,128)(2,1)}, bf16[3,4,80,960]{3,2,1,0:T(8,128)(2,1)S(1)}, u32[]{:S(2)}, u32[]{:S(2)}) collective-permute-start(bf16[3,4,80,960]{3,2,1,0:T(8,128)(2,1)} %pad_maximum_fusion.refs_2_), channel_id=1, source_target_pairs={{0,64},{1,17},{2,66},{3,19},{4,68},{5,21},{6,70},{7,23},{8,72},{9,... | collective-permute-start | bytes 5529608 | tf_op jit(solution)/shard_map/ppermute | solution.py:49
  146.2 7.9 %collective-permute-start.20 = (bf16[256,960]{1,0:T(8,128)(2,1)}, bf16[256,960]{1,0:T(8,128)(2,1)}, u32[]{:S(2)}, u32[]{:S(2)}) collective-permute-start(bf16[256,960]{1,0:T(8,128)(2,1)} %slice.441), channel_id=1, source_target_pairs={{0,1},{1,0},{2,3},{3,2},{4,5},{5,4},{6,7},{7,6},{8,9},{9,8},{10,11... | collective-permute-start | bytes 1474568 | tf_op jit(solution)/shard_map/ppermute | solution.py:49
  147.7 8.0 %collective-permute-start.19 = (bf16[256,960]{1,0:T(8,128)(2,1)}, bf16[256,960]{1,0:T(8,128)(2,1)}, u32[]{:S(2)}, u32[]{:S(2)}) collective-permute-start(bf16[256,960]{1,0:T(8,128)(2,1)} %slice.442), channel_id=1, source_target_pairs={{0,1},{1,0},{2,3},{3,2},{4,5},{5,4},{6,7},{7,6},{8,9},{9,8},{10,11... | collective-permute-start | bytes 1474568 | tf_op jit(solution)/shard_map/ppermute | solution.py:49
  150.6 45.6 %collective-permute-start.33 = (bf16[3,4,80,960]{3,2,1,0:T(8,128)(2,1)}, bf16[3,4,80,960]{3,2,1,0:T(8,128)(2,1)}, u32[]{:S(2)}, u32[]{:S(2)}) collective-permute-start(bf16[3,4,80,960]{3,2,1,0:T(8,128)(2,1)} %copy-done.14), channel_id=1, source_target_pairs={{0,96},{1,25},{2,98},{3,27},{4,100},{5,29},{6,102},{7,31},{8,104},... | collective-permute-start | bytes 5529608 | tf_op jit(solution)/shard_map/ppermute | solution.py:49
  152.7 47.2 %collective-permute-start.32 = (bf16[3,4,80,960]{3,2,1,0:T(8,128)(2,1)}, bf16[3,4,80,960]{3,2,1,0:T(8,128)(2,1)}, u32[]{:S(2)}, u32[]{:S(2)}) collective-permute-start(bf16[3,4,80,960]{3,2,1,0:T(8,128)(2,1)} %copy-done.13), channel_id=1, source_target_pairs={{0,32},{1,9},{2,34},{3,11},{4,36},{5,13},{6,38},{7,15},{8,40},{9,1... | collective-permute-start | bytes 5529608 | tf_op jit(solution)/shard_map/ppermute | solution.py:49
  152.7 47.2 %collective-permute-start.34 = (bf16[3,4,80,960]{3,2,1,0:T(8,128)(2,1)}, bf16[3,4,80,960]{3,2,1,0:T(8,128)(2,1)}, u32[]{:S(2)}, u32[]{:S(2)}) collective-permute-start(bf16[3,4,80,960]{3,2,1,0:T(8,128)(2,1)} %copy-done.15), channel_id=1, source_target_pairs={{0,64},{1,17},{2,66},{3,19},{4,68},{5,21},{6,70},{7,23},{8,72},{9,... | collective-permute-start | bytes 5529608 | tf_op jit(solution)/shard_map/ppermute | solution.py:49
  177.7 33.4 %collective-permute-start.21 = (bf16[17,80,960]{2,1,0:T(8,128)(2,1)}, bf16[17,80,960]{2,1,0:T(8,128)(2,1)}, u32[]{:S(2)}, u32[]{:S(2)}) collective-permute-start(bf16[17,80,960]{2,1,0:T(8,128)(2,1)} %get-tuple-element.39), channel_id=1, source_target_pairs={{0,1},{1,0},{2,3},{3,2},{4,5},{5,4},{6,7},{7,6},{8,9},{9,8},{10,11... | collective-permute-start | bytes 7833608 | tf_op jit(solution)/shard_map/ppermute | solution.py:49
  206.3 10.4 %collective-permute-start.37 = (bf16[3,80,960]{2,1,0:T(8,128)(2,1)S(1)}, bf16[3,80,960]{2,1,0:T(8,128)(2,1)S(1)}, u32[]{:S(2)}, u32[]{:S(2)}) collective-permute-start(bf16[3,80,960]{2,1,0:T(8,128)(2,1)S(1)} %get-tuple-element.73), channel_id=1, source_target_pairs={{0,16},{1,65},{2,18},{3,67},{4,20},{5,69},{6,22},{7,71},{8,24},{9,... | collective-permute-start | bytes 1382408 | tf_op jit(solution)/shard_map/ppermute | solution.py:49
  209.1 24.0 %collective-permute-start.36 = (bf16[3,80,960]{2,1,0:T(8,128)(2,1)}, bf16[3,80,960]{2,1,0:T(8,128)(2,1)}, u32[]{:S(2)}, u32[]{:S(2)}) collective-permute-start(bf16[3,80,960]{2,1,0:T(8,128)(2,1)} %get-tuple-element.74), channel_id=1, source_target_pairs={{0,24},{1,97},{2,26},{3,99},{4,28},{5,101},{6,30},{7,103},{8,0},{9... | collective-permute-start | bytes 1382408 | tf_op jit(solution)/shard_map/ppermute | solution.py:49
  211.1 22.0 %collective-permute-start.35 = (bf16[3,80,960]{2,1,0:T(8,128)(2,1)}, bf16[3,80,960]{2,1,0:T(8,128)(2,1)}, u32[]{:S(2)}, u32[]{:S(2)}) collective-permute-start(bf16[3,80,960]{2,1,0:T(8,128)(2,1)} %get-tuple-element.72), channel_id=1, source_target_pairs={{0,8},{1,33},{2,10},{3,35},{4,12},{5,37},{6,14},{7,39},{8,16},{9,4... | collective-permute-start | bytes 1382408 | tf_op jit(solution)/shard_map/ppermute | solution.py:49
  216.3 22.9 %collective-permute-start.24 = (bf16[336,960]{1,0:T(8,128)(2,1)}, bf16[336,960]{1,0:T(8,128)(2,1)}, u32[]{:S(2)}, u32[]{:S(2)}) collective-permute-start(bf16[336,960]{1,0:T(8,128)(2,1)} %get-tuple-element.112), channel_id=1, source_target_pairs={{0,64},{1,17},{2,66},{3,19},{4,68},{5,21},{6,70},{7,23},{8,72},{9,... | collective-permute-start | bytes 1935368 | tf_op jit(solution)/shard_map/ppermute | solution.py:49
  216.6 23.2 %collective-permute-start.23 = (bf16[336,960]{1,0:T(8,128)(2,1)S(1)}, bf16[336,960]{1,0:T(8,128)(2,1)}, u32[]{:S(2)}, u32[]{:S(2)}) collective-permute-start(bf16[336,960]{1,0:T(8,128)(2,1)S(1)} %get-tuple-element.111), channel_id=1, source_target_pairs={{0,96},{1,25},{2,98},{3,27},{4,100},{5,29},{6,102},{7,31},{8,104},... | collective-permute-start | bytes 1935368 | tf_op jit(solution)/shard_map/ppermute | solution.py:49
  216.7 23.1 %collective-permute-start.22 = (bf16[336,960]{1,0:T(8,128)(2,1)S(1)}, bf16[336,960]{1,0:T(8,128)(2,1)}, u32[]{:S(2)}, u32[]{:S(2)}) collective-permute-start(bf16[336,960]{1,0:T(8,128)(2,1)S(1)} %get-tuple-element.110), channel_id=1, source_target_pairs={{0,32},{1,9},{2,34},{3,11},{4,36},{5,13},{6,38},{7,15},{8,40},{9,1... | collective-permute-start | bytes 1935368 | tf_op jit(solution)/shard_map/ppermute | solution.py:49
  235.0 13.2 %collective-permute-start.40 = (bf16[3,20,960]{2,1,0:T(8,128)(2,1)S(1)}, bf16[3,20,960]{2,1,0:T(8,128)(2,1)S(1)}, u32[]{:S(2)}, u32[]{:S(2)}) collective-permute-start(bf16[3,20,960]{2,1,0:T(8,128)(2,1)S(1)} %get-tuple-element.87), channel_id=1, source_target_pairs={{0,4},{1,5},{2,6},{3,7},{4,0},{5,1},{6,2},{7,3},{8,12},{9,13},{10,... | collective-permute-start | bytes 345608 | tf_op jit(solution)/shard_map/ppermute | solution.py:49
  237.8 11.3 %collective-permute-start.39 = (bf16[3,20,960]{2,1,0:T(8,128)(2,1)S(1)}, bf16[3,20,960]{2,1,0:T(8,128)(2,1)S(1)}, u32[]{:S(2)}, u32[]{:S(2)}) collective-permute-start(bf16[3,20,960]{2,1,0:T(8,128)(2,1)S(1)} %get-tuple-element.88), channel_id=1, source_target_pairs={{0,6},{1,7},{2,0},{3,1},{4,2},{5,3},{6,4},{7,5},{8,14},{9,15},{10,... | collective-permute-start | bytes 345608 | tf_op jit(solution)/shard_map/ppermute | solution.py:49
  239.1 9.9 %collective-permute-start.38 = (bf16[3,20,960]{2,1,0:T(8,128)(2,1)S(1)}, bf16[3,20,960]{2,1,0:T(8,128)(2,1)S(1)}, u32[]{:S(2)}, u32[]{:S(2)}) collective-permute-start(bf16[3,20,960]{2,1,0:T(8,128)(2,1)S(1)} %get-tuple-element.86), channel_id=1, source_target_pairs={{0,2},{1,3},{2,4},{3,5},{4,6},{5,7},{6,0},{7,1},{8,10},{9,11},{10,... | collective-permute-start | bytes 345608 | tf_op jit(solution)/shard_map/ppermute | solution.py:49
  242.7 8.0 %collective-permute-start.27 = (bf16[96,960]{1,0:T(8,128)(2,1)S(1)}, bf16[96,960]{1,0:T(8,128)(2,1)S(1)}, u32[]{:S(2)}, u32[]{:S(2)}) collective-permute-start(bf16[96,960]{1,0:T(8,128)(2,1)S(1)} %get-tuple-element.109), channel_id=1, source_target_pairs={{0,16},{1,65},{2,18},{3,67},{4,20},{5,69},{6,22},{7,71},{8,24},{9,... | collective-permute-start | bytes 552968 | tf_op jit(solution)/shard_map/ppermute | solution.py:49
  (72 other events, 262.1 us)
